TPU v7x, 32 devices: a whole 2x2x4 slice. The times are simulated.
32 devices in a mesh: groups: 2 (over y), rows: 4 (over z), shard: 4 (over x, core).
Axes of the slice: x: 2, y: 2, z: 4, core: 2. Of those that a mesh axis runs over, the one named last changes fastest.
Arguments:
- images: bfloat16 [8, 8, 128, 512], P(('groups', 'shard'), 'rows'), parts along dimension 0, may hold values from -6 to 6
- cotangent: bfloat16 [8, 8, 128, 512], P(('groups', 'shard'), 'rows'), parts along dimension 0, may hold values from -6 to 6
- weight_in: bfloat16 [2, 512, 512], P(None, 'shard'), may hold values from -0.25 to 0.25
- weight_group: bfloat16 [2, 144, 512], P(None, 'shard'), may hold values from -0.5 to 0.5
- weight_out: bfloat16 [2, 512, 512], P(None, 'shard'), may hold values from -0.25 to 0.25
Outputs:
- decoded: bfloat16 [8, 8, 128, 512], P(('groups', 'shard'), 'rows'), parts along dimension 0
- grad_images: bfloat16 [8, 8, 128, 512], P(('groups', 'shard'), 'rows'), parts along dimension 0
- grad_in: float32 [4, 512, 512], P('groups', 'shard'), parts along dimension 0
- grad_group: float32 [4, 144, 512], P('groups', 'shard'), parts along dimension 0
- grad_out: float32 [4, 512, 512], P('groups', 'shard'), parts along dimension 0
There are 2 independent parts, one for each index of `groups`. A program takes and returns all parts, laid end to end along the dimension named above; an argument that names none is the same for every part. Nothing has to cross between parts.
All inputs are finite; a program needn't handle non-finite values.
Results may differ from a plain program's by a relative error of at most 0.02.
Values may be sent and summed in bfloat16 or wider, within the bound.
A program may use at most 128 MiB of HBM per device.

v0:
```python
import math
import jax
import jax.numpy as jnp
from jax import lax
from jax.sharding import PartitionSpec as P

GW = 16


def extended_2(cells, sides, width):
    for axis, dim in sides:
        count = lax.axis_size(axis)
        ends = count - 1
        head = lax.slice_in_dim(cells, 0, width, axis=dim)
        tail = lax.slice_in_dim(cells, cells.shape[dim] - width, cells.shape[dim], axis=dim)
        cells = jnp.concatenate(
            [
                lax.ppermute(tail, axis, [(i, (i + 1) % count) for i in range(ends)]),
                cells,
                lax.ppermute(head, axis, [((i + 1) % count, i) for i in range(ends)]),
            ],
            axis=dim,
        )
    return cells


def silu_slope(preact):
    sigmoid_value = jax.nn.sigmoid(preact)
    return sigmoid_value * (1.0 + preact * (1.0 - sigmoid_value))


def block_kernel(full_group, hidden_width, group_width):
    sub_width = min(hidden_width, 128)
    sections = hidden_width // sub_width
    members = sub_width // group_width
    arranged = full_group.reshape(9, group_width, sections, members, group_width)
    arranged = arranged.transpose(0, 2, 3, 1, 4)
    identity = jnp.eye(members, dtype=full_group.dtype)
    expanded = arranged[:, :, :, :, None, :] * identity[None, None, :, None, :, None]
    return expanded.reshape(9, sections, sub_width, sub_width)


def grouped_taps(padded, kernel, out_rows, out_cols, flipped, pattern):
    summed = None
    for tap_index in range(9):
        row_step = tap_index // 3
        col_step = tap_index % 3
        if flipped:
            row_step = 2 - row_step
            col_step = 2 - col_step
        window = padded[:, row_step : row_step + out_rows, col_step : col_step + out_cols, :]
        window = window.reshape(-1, kernel.shape[1], kernel.shape[2])
        tap_term = jnp.einsum(
            pattern, window, kernel[tap_index], preferred_element_type=jnp.float32
        )
        summed = tap_term if summed is None else summed + tap_term
    return summed


def body(images, cotangent, weight_in, weight_group, weight_out):
    tile_count, height, across, channels = images.shape
    block_count = weight_in.shape[0]
    group_width = GW
    pixels = tile_count * height * across
    current = images.reshape(pixels, channels)
    stored = []
    for block_index in range(block_count):
        full_in, full_group, full_out = (
            lax.all_gather(weight_in[block_index], "shard", axis=0, tiled=True),
            lax.all_gather(weight_group[block_index], "shard", axis=0, tiled=True),
            lax.all_gather(weight_out[block_index], "shard", axis=0, tiled=True),
        )
        hidden_width = full_in.shape[1]
        kernel = block_kernel(full_group, hidden_width, group_width)
        pre_one = jnp.dot(current, full_in, preferred_element_type=jnp.float32)
        hidden_one = (
            jax.nn.silu(pre_one)
            .astype(jnp.bfloat16)
            .reshape(tile_count, height, across, hidden_width)
        )
        haloed = extended_2(hidden_one, (("rows", 1),), 1)
        padded_one = jnp.pad(haloed, ((0, 0), (0, 0), (1, 1), (0, 0)))
        pre_two = grouped_taps(padded_one, kernel, height, across, False, "psi,sio->pso").reshape(
            pixels, hidden_width
        )
        hidden_two = jax.nn.silu(pre_two).astype(jnp.bfloat16)
        pre_three = current.astype(jnp.float32) + jnp.dot(
            hidden_two, full_out, preferred_element_type=jnp.float32
        )
        kept_weights = None
        stored.append((current, pre_one, padded_one, pre_two, hidden_two, pre_three, kept_weights))
        current = jax.nn.silu(pre_three).astype(jnp.bfloat16)
    decoded = current.reshape(images.shape)
    grad_flow = cotangent.reshape(pixels, channels)
    shares = []
    for block_index in reversed(range(block_count)):
        flow_in, pre_one, padded_one, pre_two, hidden_two, pre_three, kept_weights = stored[
            block_index
        ]
        full_in, full_group, full_out = (
            lax.all_gather(weight_in[block_index], "shard", axis=0, tiled=True),
            lax.all_gather(weight_group[block_index], "shard", axis=0, tiled=True),
            lax.all_gather(weight_out[block_index], "shard", axis=0, tiled=True),
        )
        hidden_width = full_in.shape[1]
        kernel = block_kernel(full_group, hidden_width, group_width)
        sections = kernel.shape[1]
        sub_width = kernel.shape[2]
        members = sub_width // group_width
        slope_three = grad_flow.astype(jnp.float32) * silu_slope(pre_three)
        low_three = slope_three.astype(jnp.bfloat16)
        part_out = jnp.einsum(
            "pw,pc->wc", hidden_two, low_three, preferred_element_type=jnp.float32
        )
        slope_two = (
            jnp.einsum("pc,wc->pw", low_three, full_out, preferred_element_type=jnp.float32)
            * silu_slope(pre_two)
        ).astype(jnp.bfloat16)
        slope_sections = slope_two.reshape(pixels, sections, sub_width)
        tap_terms = []
        for tap_index in range(9):
            row_step = tap_index // 3
            col_step = tap_index % 3
            window = padded_one[:, row_step : row_step + height, col_step : col_step + across, :]
            window = window.reshape(pixels, sections, sub_width)
            blockwise = jnp.einsum(
                "psi,pso->sio", window, slope_sections, preferred_element_type=jnp.float32
            )
            blockwise = blockwise.reshape(sections, members, group_width, members, group_width)
            same = jnp.eye(members, dtype=jnp.float32)[None, :, None, :, None]
            diagonal_part = jnp.sum(blockwise * same, axis=1)
            tap_terms.append(diagonal_part.transpose(1, 0, 2, 3).reshape(group_width, hidden_width))
        part_group = jnp.stack(tap_terms).reshape(9 * group_width, hidden_width)
        slope_grid = slope_two.reshape(tile_count, height, across, hidden_width)
        padded_slope = jnp.pad(slope_grid, ((0, 0), (2, 2), (1, 1), (0, 0)))
        extended = grouped_taps(padded_slope, kernel, height + 2, across, True, "pso,sio->psi")
        extended = extended.reshape(tile_count, height + 2, across, hidden_width)
        edge_rows = jnp.concatenate([extended[:, :1], extended[:, -1:]], axis=1)
        borders = extended_2(edge_rows.astype(jnp.bfloat16), (("rows", 1),), 1).astype(
            edge_rows.dtype
        )
        back_one = extended[:, 1:-1]
        back_one = back_one.at[:, :1].add(borders[:, :1])
        back_one = back_one.at[:, -1:].add(borders[:, -1:])
        slope_one = (back_one.reshape(pixels, hidden_width) * silu_slope(pre_one)).astype(
            jnp.bfloat16
        )
        part_in = jnp.einsum("pc,pw->cw", flow_in, slope_one, preferred_element_type=jnp.float32)
        grad_flow = (
            slope_three
            + jnp.einsum("pw,cw->pc", slope_one, full_in, preferred_element_type=jnp.float32)
        ).astype(jnp.bfloat16)
        shares.append(
            (
                lax.psum_scatter(
                    part_in.astype(jnp.bfloat16), "shard", scatter_dimension=0, tiled=True
                ).astype(jnp.float32),
                lax.psum_scatter(
                    part_group.astype(jnp.bfloat16), "shard", scatter_dimension=0, tiled=True
                ).astype(jnp.float32),
                lax.psum_scatter(
                    part_out.astype(jnp.bfloat16), "shard", scatter_dimension=0, tiled=True
                ).astype(jnp.float32),
            )
        )
    shares = shares[::-1]
    totals = (
        lax.psum(jnp.stack([entry[0] for entry in shares]).astype(jnp.bfloat16), "rows").astype(
            jnp.float32
        ),
        lax.psum(jnp.stack([entry[1] for entry in shares]).astype(jnp.bfloat16), "rows").astype(
            jnp.float32
        ),
        lax.psum(jnp.stack([entry[2] for entry in shares]).astype(jnp.bfloat16), "rows").astype(
            jnp.float32
        ),
    )
    norm_factor = 1.0 / math.sqrt(pixels * lax.axis_size("rows") * lax.axis_size("shard"))
    grad_images = grad_flow.reshape(images.shape)
    return (
        decoded,
        grad_images,
        totals[0] * norm_factor,
        totals[1] * norm_factor,
        totals[2] * norm_factor,
    )


def solution(mesh):
    placed = (
        P(("groups", "shard"), "rows", None, None),
        P(("groups", "shard"), "rows", None, None),
        P(None, "shard", None),
        P(None, "shard", None),
        P(None, "shard", None),
    )
    return jax.shard_map(
        body,
        mesh=mesh,
        in_specs=placed,
        out_specs=(
            P(("groups", "shard"), "rows", None, None),
            P(("groups", "shard"), "rows", None, None),
            P("groups", "shard", None),
            P("groups", "shard", None),
            P("groups", "shard", None),
        ),
        check_vma=False,
    )
```

profile of v0, /device:TPU:0, one launch (start us, length us, event | category | flops | bytes accessed | tf_op | source)
XLA Modules:
  0.0 473.4 jit_solution(3516267203745144367)
XLA Ops:
  8.9 8.6 %all-gather.1 = bf16[1,512,512]{2,1,0:T(8,128)(2,1)S(1)} all-gather(bf16[1,128,512]{2,1,0:T(8,128)(2,1)S(1)} %get-tuple-element.160), channel_id=3, replica_groups=mesh['groups'=2,'rows'=4,'shard'=4] {'shard'}, dimensions={1}, use_global_device_ids=true | all-gather | bytes 655360 | tf_op jit(solution)/shard_map/all_gather | solution.py:69
  18.3 2.1 multiply_convert_fusion.5
  22.4 5.2 %collective-permute-start = (bf16[1,1,128,512]{3,2,1,0:T(8,128)(2,1)}, bf16[1,1,128,512]{3,2,1,0:T(8,128)(2,1)}, u32[]{:S(2)}, u32[]{:S(2)}) collective-permute-start(bf16[1,1,128,512]{3,2,1,0:T(8,128)(2,1)} %get-tuple-element.158), channel_id=1, source_target_pairs={{0,4},{4,8},{8,12},{1,5},{5,9},{9,13},{2,6},{6,10},{10,14},{3,7},{... | collective-permute-start | bytes 393224 | tf_op jit(solution)/shard_map/ppermute | solution.py:18
  29.4 5.9 %all-gather = bf16[1,144,512]{2,0,1:T(2,128)(2,1)S(1)} all-gather(bf16[1,36,512]{2,0,1:T(2,128)(2,1)S(1)} %get-tuple-element.164), channel_id=2, replica_groups=mesh['groups'=2,'rows'=4,'shard'=4] {'shard'}, dimensions={1}, use_global_device_ids=true | all-gather | bytes 184320 | tf_op jit(solution)/shard_map/all_gather | solution.py:70
  38.4 6.0 %all-gather.3 = bf16[1,144,512]{2,0,1:T(2,128)(2,1)S(1)} all-gather(bf16[1,36,512]{2,0,1:T(2,128)(2,1)S(1)} %get-tuple-element.165), channel_id=5, replica_groups=mesh['groups'=2,'rows'=4,'shard'=4] {'shard'}, dimensions={1}, use_global_device_ids=true | all-gather | bytes 184320 | tf_op jit(solution)/shard_map/all_gather | solution.py:70
  47.7 9.4 %all-gather.4 = bf16[1,512,512]{2,1,0:T(8,128)(2,1)} all-gather(bf16[1,128,512]{2,1,0:T(8,128)(2,1)} %get-tuple-element.161), channel_id=6, replica_groups=mesh['groups'=2,'rows'=4,'shard'=4] {'shard'}, dimensions={1}, use_global_device_ids=true | all-gather | bytes 655360 | tf_op jit(solution)/shard_map/all_gather | solution.py:69
  57.0 4.3 broadcast_multiply_fusion.1
  61.4 8.6 %fusion.110 = (bf16[1,4,8,16,8,16]{3,2,5,4,1,0:T(8,128)(2,1)S(1)}, bf16[1,4,8,16,8,16]{3,2,5,4,1,0:T(8,128)(2,1)S(1)}, bf16[1,4,8,16,8,16]{3,2,5,4,1,0:T(8,128)(...) fusion(bf16[9,4,8,16,8,16]{3,2,5,4,1,0:T(8,128)(2,1)} %get-tupl, ...), kind=kLoop, calls=%fused_computation.267 | loop fusion | bytes 4718592 | tf_op jit(solution)/shard_map/slice | solution.py:54
  70.0 2.0 squeeze.97
  72.0 2.6 squeeze.99
  74.6 2.6 squeeze.100
  77.2 2.6 squeeze.101
  79.8 2.6 squeeze.102
  82.4 2.6 squeeze.103
  85.0 2.6 squeeze.104
  87.7 2.6 squeeze.105
  90.3 2.6 squeeze.106
  92.9 8.8 %all-gather.2 = bf16[1,512,512]{2,1,0:T(8,128)(2,1)} all-gather(bf16[1,128,512]{2,1,0:T(8,128)(2,1)} %get-tuple-element.162), channel_id=4, replica_groups=mesh['groups'=2,'rows'=4,'shard'=4] {'shard'}, dimensions={1}, use_global_device_ids=true | all-gather | bytes 655360 | tf_op jit(solution)/shard_map/all_gather | solution.py:71
  137.8 2.1 copy.447
  144.7 5.2 %collective-permute-start.2 = (bf16[1,1,128,512]{3,2,1,0:T(8,128)(2,1)}, bf16[1,1,128,512]{3,2,1,0:T(8,128)(2,1)}, u32[]{:S(2)}, u32[]{:S(2)}) collective-permute-start(bf16[1,1,128,512]{3,2,1,0:T(8,128)(2,1)} %get-tuple-element.154), channel_id=1, source_target_pairs={{0,4},{4,8},{8,12},{1,5},{5,9},{9,13},{2,6},{6,10},{10,14},{3,7},{... | collective-permute-start | bytes 393224 | tf_op jit(solution)/shard_map/ppermute | solution.py:18
  149.9 7.2 %all-gather.5 = bf16[1,512,512]{2,1,0:T(8,128)(2,1)} all-gather(bf16[1,128,512]{2,1,0:T(8,128)(2,1)S(1)} %copy-done.94), channel_id=7, replica_groups=mesh['groups'=2,'rows'=4,'shard'=4] {'shard'}, dimensions={1}, use_global_device_ids=true | all-gather | bytes 655360 | tf_op jit(solution)/shard_map/all_gather | solution.py:71
  157.1 2.6 squeeze.109
  159.7 2.6 squeeze.111
  162.3 2.6 squeeze.112
  164.9 2.6 squeeze.113
  167.5 2.6 squeeze.114
  170.1 2.8 squeeze.115
  185.2 2.7 convert_multiply_fusion
  206.9 2.0 reshape.661
  208.9 2.0 reshape.662
  222.8 5.2 %collective-permute-start.4 = (bf16[1,1,128,512]{3,2,1,0:T(8,128)(2,1)}, bf16[1,1,128,512]{3,2,1,0:T(8,128)(2,1)}, u32[]{:S(2)}, u32[]{:S(2)}) collective-permute-start(bf16[1,1,128,512]{3,2,1,0:T(8,128)(2,1)} %copy.459), channel_id=1, source_target_pairs={{0,4},{4,8},{8,12},{1,5},{5,9},{9,13},{2,6},{6,10},{10,14},{3,7},{... | collective-permute-start | bytes 393224 | tf_op jit(solution)/shard_map/ppermute | solution.py:18
  236.9 2.0 reshape.696
  240.8 2.0 reshape.698
  260.7 2.3 pad_slice_fusion
  273.1 2.0 reshape.674
  279.0 2.0 reshape.677
  294.0 5.3 %collective-permute-start.6 = (bf16[1,1,128,512]{3,2,1,0:T(8,128)(2,1)}, bf16[1,1,128,512]{3,2,1,0:T(8,128)(2,1)}, u32[]{:S(2)}, u32[]{:S(2)}) collective-permute-start(bf16[1,1,128,512]{3,2,1,0:T(8,128)(2,1)} %copy.463), channel_id=1, source_target_pairs={{0,4},{4,8},{8,12},{1,5},{5,9},{9,13},{2,6},{6,10},{10,14},{3,7},{... | collective-permute-start | bytes 393224 | tf_op jit(solution)/shard_map/ppermute | solution.py:18
  301.3 2.9 reshape.683
  306.1 2.9 reshape.685
  311.0 3.0 reshape.687
  315.8 2.9 reshape.689
  320.6 15.7 %multiply_reduce_fusion.9 = (bf16[4,16,8,16]{3,2,1,0:T(8,128)(2,1)}, bf16[4,16,8,16]{3,2,1,0:T(8,128)(2,1)}, bf16[4,16,8,16]{3,2,1,0:T(8,128)(2,1)S(1)}, bf16[4,...) fusion(f32[4,8,16,8,16]{4,3,2,1,0:T(8,128)} %reshape.690, ...), kind=kLoop, calls=%fused_computation.29 | loop fusion | flops 2211840 | bytes 5013760 | tf_op jit(solution)/shard_map/reduce_sum | solution.py:131
  343.6 2.3 convolution_convert_fusion.2
  360.8 9.3 %fusion.109 = (bf16[40,512]{1,0:T(8,128)(2,1)S(1)}, bf16[40,512]{1,0:T(8,128)(2,1)S(1)}) fusion(bf16[144,512]{1,0:T(8,128)(2,1)S(1)} %bitcast.538, bf16[144,512]{1,0:T(8,128)(2,1)} %bitcast.42), kind=kCustom, calls=%all-reduce-scatter.2 | all-reduce-scatter fusion | flops 163841 | bytes 377344
  371.6 4.3 collective-permute-start.8
  380.3 13.7 %reduce-scatter.21.cloned.1.call-done = bf16[128,512]{1,0:T(8,128)(2,1)} async-done(((bf16[512,512]{1,0:T(8,128)(2,1)}), bf16[128,512]{1,0:T(8,128)(2,1)}) %reduce-scatter.21.cloned.1.call-update) | async-done | bytes 131088
  395.8 23.0 %reduce-scatter.17.cloned.1.call-done = bf16[128,512]{1,0:T(8,128)(2,1)} async-done(((bf16[512,512]{1,0:T(8,128)(2,1)}), bf16[128,512]{1,0:T(8,128)(2,1)}) %reduce-scatter.17.cloned.1.call-update) | async-done | bytes 131088
  421.6 40.3 %all-reduce.12.cloned.1.call-done = (bf16[2,128,512]{1,2,0:T(8,128)(2,1)}, bf16[2,36,512]{2,1,0:T(8,128)(2,1)}, bf16[2,128,512]{1,2,0:T(8,128)(2,1)}) async-done(((bf16[2,128,512]{1,2,0:T(8,128)(2,1)}, bf16[2,36,512]{2,1,0:T(8,128)(2,1)}, bf16[2,128,512]{1,2,0:T(8,128)(2,1)}), (bf16[2,128,512]{1,2,0:T(8,128)(2,1)}, bf16[2,36,512]{2,1,0:T(8,128)(2,1)}, ...) | async-done | bytes 598032 | tf_op jit(solution)/shard_map/psum | solution.py:168
  (510 shorter events, 197.0 us)
Async XLA Ops:
  7.2 371.0 %reduce-scatter.23.cloned.1.call-start = ((), (), s32[]{:S(2)}) async-start(), calls=%async_computation.7 | async-start | bytes 655360
  17.5 11.0 %copy-start.108 = (bf16[2,128,512]{2,1,0:T(8,128)(2,1)S(1)}, bf16[2,128,512]{2,1,0:T(8,128)(2,1)}, u32[]{:S(2)}) copy-start(bf16[2,128,512]{2,1,0:T(8,128)(2,1)} %param.17) | copy-start | bytes 786436
  18.3 11.0 %copy-start.104 = (bf16[2,36,512]{2,0,1:T(2,128)(2,1)S(1)}, bf16[2,36,512]{2,0,1:T(2,128)(2,1)}, u32[]{:S(2)}) copy-start(bf16[2,36,512]{2,0,1:T(2,128)(2,1)} %param.16) | copy-start | bytes 221188
  20.4 16.7 %copy-start = (bf16[256,512]{1,0:T(8,128)(2,1)}, bf16[256,512]{1,0:T(8,128)(2,1)S(1)}, u32[]{:S(2)}) copy-start(bf16[256,512]{1,0:T(8,128)(2,1)S(1)} %get-tuple-element.168) | copy-start | bytes 786436
  21.1 80.6 %collective-permute-start.1 = (bf16[1,1,128,512]{3,2,1,0:T(8,128)(2,1)}, bf16[1,1,128,512]{3,2,1,0:T(8,128)(2,1)}, u32[]{:S(2)}, u32[]{:S(2)}) collective-permute-start(bf16[1,1,128,512]{3,2,1,0:T(8,128)(2,1)} %get-tuple-element.159), channel_id=1, source_target_pairs={{4,0},{8,4},{12,8},{5,1},{9,5},{13,9},{6,2},{10,6},{14,10},{7,3},{... | collective-permute-start | bytes 393224 | tf_op jit(solution)/shard_map/ppermute | solution.py:20
  22.4 79.3 %collective-permute-start = (bf16[1,1,128,512]{3,2,1,0:T(8,128)(2,1)}, bf16[1,1,128,512]{3,2,1,0:T(8,128)(2,1)}, u32[]{:S(2)}, u32[]{:S(2)}) collective-permute-start(bf16[1,1,128,512]{3,2,1,0:T(8,128)(2,1)} %get-tuple-element.158), channel_id=1, source_target_pairs={{0,4},{4,8},{8,12},{1,5},{5,9},{9,13},{2,6},{6,10},{10,14},{3,7},{... | collective-permute-start | bytes 393224 | tf_op jit(solution)/shard_map/ppermute | solution.py:18
  85.0 16.7 %copy-start.1 = (bf16[256,512]{1,0:T(8,128)(2,1)S(1)}, bf16[256,512]{1,0:T(8,128)(2,1)}, u32[]{:S(2)}) copy-start(bf16[256,512]{1,0:T(8,128)(2,1)} %copy-done) | copy-start | bytes 786436
  109.3 7.1 %copy-start.80 = (bf16[1,2,128,512]{3,2,1,0:T(8,128)(2,1)S(1)}, bf16[1,2,128,512]{3,2,1,0:T(8,128)(2,1)}, u32[]{:S(2)}) copy-start(bf16[1,2,128,512]{3,2,1,0:T(8,128)(2,1)} %get-tuple-element.129) | copy-start | bytes 786436
  119.0 14.2 %copy-start.2 = (bf16[256,4,128]{0,2,1:T(8,128)(2,1)S(1)}, bf16[256,4,128]{0,2,1:T(8,128)(2,1)}, u32[]{:S(2)}) copy-start(bf16[256,4,128]{0,2,1:T(8,128)(2,1)} %copy.370) | copy-start | bytes 786436
  141.5 8.3 %copy-start.94 = (bf16[1,128,512]{2,1,0:T(8,128)(2,1)S(1)}, bf16[1,128,512]{2,1,0:T(8,128)(2,1)}, u32[]{:S(2)}) copy-start(bf16[1,128,512]{2,1,0:T(8,128)(2,1)} %get-tuple-element.163) | copy-start | bytes 393220
  143.4 32.4 %collective-permute-start.3 = (bf16[1,1,128,512]{3,2,1,0:T(8,128)(2,1)}, bf16[1,1,128,512]{3,2,1,0:T(8,128)(2,1)}, u32[]{:S(2)}, u32[]{:S(2)}) collective-permute-start(bf16[1,1,128,512]{3,2,1,0:T(8,128)(2,1)} %get-tuple-element.155), channel_id=1, source_target_pairs={{4,0},{8,4},{12,8},{5,1},{9,5},{13,9},{6,2},{10,6},{14,10},{7,3},{... | collective-permute-start | bytes 393224 | tf_op jit(solution)/shard_map/ppermute | solution.py:20
  144.7 31.1 %collective-permute-start.2 = (bf16[1,1,128,512]{3,2,1,0:T(8,128)(2,1)}, bf16[1,1,128,512]{3,2,1,0:T(8,128)(2,1)}, u32[]{:S(2)}, u32[]{:S(2)}) collective-permute-start(bf16[1,1,128,512]{3,2,1,0:T(8,128)(2,1)} %get-tuple-element.154), channel_id=1, source_target_pairs={{0,4},{4,8},{8,12},{1,5},{5,9},{9,13},{2,6},{6,10},{10,14},{3,7},{... | collective-permute-start | bytes 393224 | tf_op jit(solution)/shard_map/ppermute | solution.py:18
  174.9 8.8 %copy-start.52 = (bf16[4,128,128]{1,2,0:T(8,128)(2,1)}, bf16[4,128,128]{1,2,0:T(8,128)(2,1)S(1)}, u32[]{:S(2)}) copy-start(bf16[4,128,128]{1,2,0:T(8,128)(2,1)S(1)} %squeeze.117) | copy-start | bytes 393220
  175.6 8.3 %copy-start.50 = (bf16[4,128,128]{1,2,0:T(8,128)(2,1)}, bf16[4,128,128]{1,2,0:T(8,128)(2,1)S(1)}, u32[]{:S(2)}) copy-start(bf16[4,128,128]{1,2,0:T(8,128)(2,1)S(1)} %squeeze.118) | copy-start | bytes 393220
  187.9 7.8 %copy-start.114 = (f32[256,512]{1,0:T(8,128)}, f32[256,512]{1,0:T(8,128)S(1)}, u32[]{:S(2)}) copy-start(f32[256,512]{1,0:T(8,128)S(1)} %get-tuple-element.132) | copy-start | bytes 1572868
  220.7 27.2 %collective-permute-start.5 = (bf16[1,1,128,512]{3,2,1,0:T(8,128)(2,1)}, bf16[1,1,128,512]{3,2,1,0:T(8,128)(2,1)}, u32[]{:S(2)}, u32[]{:S(2)}) collective-permute-start(bf16[1,1,128,512]{3,2,1,0:T(8,128)(2,1)} %copy.460), channel_id=1, source_target_pairs={{4,0},{8,4},{12,8},{5,1},{9,5},{13,9},{6,2},{10,6},{14,10},{7,3},{... | collective-permute-start | bytes 393224 | tf_op jit(solution)/shard_map/ppermute | solution.py:20
  222.0 8.5 %copy-start.66 = (f32[4,128,128]{2,1,0:T(8,128)S(1)}, f32[4,128,128]{2,1,0:T(8,128)}, u32[]{:S(2)}) copy-start(f32[4,128,128]{2,1,0:T(8,128)} %fusion.61) | copy-start | bytes 786436
  222.8 25.1 %collective-permute-start.4 = (bf16[1,1,128,512]{3,2,1,0:T(8,128)(2,1)}, bf16[1,1,128,512]{3,2,1,0:T(8,128)(2,1)}, u32[]{:S(2)}, u32[]{:S(2)}) collective-permute-start(bf16[1,1,128,512]{3,2,1,0:T(8,128)(2,1)} %copy.459), channel_id=1, source_target_pairs={{0,4},{4,8},{8,12},{1,5},{5,9},{9,13},{2,6},{6,10},{10,14},{3,7},{... | collective-permute-start | bytes 393224 | tf_op jit(solution)/shard_map/ppermute | solution.py:18
  246.7 132.6 %reduce-scatter.19.cloned.1.call-start = ((), (), s32[]{:S(2)}) async-start(), calls=%async_computation.5 | async-start | bytes 655360
  252.5 4.6 copy-start.12
  253.4 4.6 copy-start.14
  254.3 4.6 copy-start.16
  255.2 4.6 copy-start.3
  273.1 7.9 %copy-start.49 = (bf16[4,128,128]{1,2,0:T(8,128)(2,1)S(1)}, bf16[4,128,128]{1,2,0:T(8,128)(2,1)}, u32[]{:S(2)}) copy-start(bf16[4,128,128]{1,2,0:T(8,128)(2,1)} %squeeze.99) | copy-start | bytes 393220
  287.1 12.2 %copy-start.74 = (f32[4,128,128]{2,1,0:T(8,128)S(1)}, f32[4,128,128]{2,1,0:T(8,128)}, u32[]{:S(2)}) copy-start(f32[4,128,128]{2,1,0:T(8,128)} %fusion.63) | copy-start | bytes 786436
  291.0 63.8 %collective-permute-start.7 = (bf16[1,1,128,512]{3,2,1,0:T(8,128)(2,1)S(1)}, bf16[1,1,128,512]{3,2,1,0:T(8,128)(2,1)}, u32[]{:S(2)}, u32[]{:S(2)}) collective-permute-start(bf16[1,1,128,512]{3,2,1,0:T(8,128)(2,1)S(1)} %copy.464), channel_id=1, source_target_pairs={{4,0},{8,4},{12,8},{5,1},{9,5},{13,9},{6,2},{10,6},{14,10},{7,3},{... | collective-permute-start | bytes 393224 | tf_op jit(solution)/shard_map/ppermute | solution.py:20
  294.0 60.8 %collective-permute-start.6 = (bf16[1,1,128,512]{3,2,1,0:T(8,128)(2,1)}, bf16[1,1,128,512]{3,2,1,0:T(8,128)(2,1)}, u32[]{:S(2)}, u32[]{:S(2)}) collective-permute-start(bf16[1,1,128,512]{3,2,1,0:T(8,128)(2,1)} %copy.463), channel_id=1, source_target_pairs={{0,4},{4,8},{8,12},{1,5},{5,9},{9,13},{2,6},{6,10},{10,14},{3,7},{... | collective-permute-start | bytes 393224 | tf_op jit(solution)/shard_map/ppermute | solution.py:18
  336.3 4.9 %copy-start.103 = (bf16[4,16,8,16]{3,2,1,0:T(8,128)(2,1)S(1)}, bf16[4,16,8,16]{3,2,1,0:T(8,128)(2,1)}, u32[]{:S(2)}) copy-start(bf16[4,16,8,16]{3,2,1,0:T(8,128)(2,1)} %get-tuple-element.86) | copy-start | bytes 49156
  336.3 5.1 %copy-start.102 = (bf16[4,16,8,16]{3,2,1,0:T(8,128)(2,1)S(1)}, bf16[4,16,8,16]{3,2,1,0:T(8,128)(2,1)}, u32[]{:S(2)}) copy-start(bf16[4,16,8,16]{3,2,1,0:T(8,128)(2,1)} %get-tuple-element.87) | copy-start | bytes 49156
  336.3 5.3 %copy-start.101 = (bf16[4,16,8,16]{3,2,1,0:T(8,128)(2,1)S(1)}, bf16[4,16,8,16]{3,2,1,0:T(8,128)(2,1)}, u32[]{:S(2)}) copy-start(bf16[4,16,8,16]{3,2,1,0:T(8,128)(2,1)} %get-tuple-element.88) | copy-start | bytes 49156
  336.3 5.5 %copy-start.100 = (bf16[4,16,8,16]{3,2,1,0:T(8,128)(2,1)S(1)}, bf16[4,16,8,16]{3,2,1,0:T(8,128)(2,1)}, u32[]{:S(2)}) copy-start(bf16[4,16,8,16]{3,2,1,0:T(8,128)(2,1)} %get-tuple-element.89) | copy-start | bytes 49156
  336.3 5.8 %copy-start.99 = (bf16[4,16,8,16]{3,2,1,0:T(8,128)(2,1)S(1)}, bf16[4,16,8,16]{3,2,1,0:T(8,128)(2,1)}, u32[]{:S(2)}) copy-start(bf16[4,16,8,16]{3,2,1,0:T(8,128)(2,1)} %get-tuple-element.90) | copy-start | bytes 49156
  336.3 6.0 %copy-start.98 = (bf16[4,16,8,16]{3,2,1,0:T(8,128)(2,1)S(1)}, bf16[4,16,8,16]{3,2,1,0:T(8,128)(2,1)}, u32[]{:S(2)}) copy-start(bf16[4,16,8,16]{3,2,1,0:T(8,128)(2,1)} %get-tuple-element.74) | copy-start | bytes 49156
  337.7 5.0 %copy-start.97 = (bf16[4,16,8,16]{3,2,1,0:T(8,128)(2,1)S(1)}, bf16[4,16,8,16]{3,2,1,0:T(8,128)(2,1)}, u32[]{:S(2)}) copy-start(bf16[4,16,8,16]{3,2,1,0:T(8,128)(2,1)} %get-tuple-element.76) | copy-start | bytes 49156
  338.9 4.7 copy-start.106
  342.7 4.8 %copy-start.93 = (bf16[1,1,128,512]{3,2,1,0:T(8,128)(2,1)S(1)}, bf16[1,1,128,512]{3,2,1,0:T(8,128)(2,1)}, u32[]{:S(2)}) copy-start(bf16[1,1,128,512]{3,2,1,0:T(8,128)(2,1)} %copy.463) | copy-start | bytes 393220
  343.6 4.0 copy-start.90
  345.9 48.1 %reduce-scatter.21.cloned.1.call-start = ((), (), s32[]{:S(2)}) async-start(), calls=%async_computation.6 | async-start | bytes 655360
  349.3 4.3 copy-start.96
  349.6 4.3 copy-start.95
  351.4 5.4 %copy-start.88 = (f32[256,512]{1,0:T(8,128)S(1)}, f32[256,512]{1,0:T(8,128)}, u32[]{:S(2)}) copy-start(f32[256,512]{1,0:T(8,128)} %get-tuple-element.169) | copy-start | bytes 1572868
  354.2 64.6 %reduce-scatter.17.cloned.1.call-start = ((), (), s32[]{:S(2)}) async-start(), calls=%async_computation.4 | async-start | bytes 655360
  356.7 4.1 copy-start.111
  356.8 19.2 %copy-start.112 = (u32[32]{0:T(128)S(1)}, u32[32]{0:T(128)}, u32[]{:S(2)}) copy-start(u32[32]{0:T(128)} %constant.124) | copy-start | bytes 388
  358.3 62.3 %copy-start.20 = (bf16[1,512,512]{2,1,0:T(8,128)(2,1)S(1)}, bf16[1,512,512]{2,1,0:T(8,128)(2,1)}, u32[]{:S(2)}) copy-start(bf16[1,512,512]{2,1,0:T(8,128)(2,1)} %copy-done.19) | copy-start | bytes 1572868
  358.3 103.6 %all-reduce.12.cloned.1.call-start = ((), (), s32[]{:S(2)}) async-start(), calls=%async_computation.8 | async-start | bytes 1212416 | tf_op jit(solution)/shard_map/psum | solution.py:168
  370.1 7.0 %collective-permute-start.9 = (bf16[12,512]{1,0:T(8,128)(2,1)S(1)}, bf16[12,512]{1,0:T(8,128)(2,1)S(1)}, u32[]{:S(2)}, u32[]{:S(2)}) collective-permute-start(bf16[12,512]{1,0:T(8,128)(2,1)S(1)} %slice.537), channel_id=1, source_target_pairs={{0,1},{1,2},{2,3},{4,5},{5,6},{6,7},{8,9},{9,10},{10,11},{12,13},{... | collective-permute-start | bytes 36872
  371.6 5.7 %collective-permute-start.8 = (bf16[12,512]{1,0:T(8,128)(2,1)S(1)}, bf16[12,512]{1,0:T(8,128)(2,1)S(1)}, u32[]{:S(2)}, u32[]{:S(2)}) collective-permute-start(bf16[12,512]{1,0:T(8,128)(2,1)S(1)} %slice.536), channel_id=1, source_target_pairs={{0,1},{1,2},{2,3},{4,5},{5,6},{6,7},{8,9},{9,10},{10,11},{12,13},{... | collective-permute-start | bytes 36872
  (85 other events, 170.4 us)
Sparse Core Ops, SparseCore 0:
  246.8 21.4 reduce-scatter.22
  346.0 22.7 reduce-scatter.18
  371.8 22.1 reduce-scatter.20
  397.1 21.6 reduce-scatter.16
  421.8 40.0 all-reduce.11
where the time goes:
time: 482 us; the launch traced here: 473 us
  local copies, waits for them, and re-layouts  206 us (43%)
  waiting for transfers between devices  77.2 us (16%)
  blocking collectives  55.2 us (11%)
  matrix products  49.6 us (10%)
  other arithmetic  36.9 us (8%)
  starting transfers between devices  32.2 us (7%)
  between operations  16.6 us (3%)
    reshape x52, local copies, waits for them, and re-layouts, grouped_taps(): window = window.reshape(-1, kernel.shape[1], kernel.shape[2])  60.5 us
    squeeze x18, local copies, waits for them, and re-layouts, grouped_taps(): kernel[tap_index]  41.4 us
    psum x1, waiting for transfers between devices, body(): lax.psum(jnp.stack([entry[0] for entry in shares]).astype(jnp.bfloat16),...  40.3 us
    reshape x18, local copies, waits for them, and re-layouts, body(): blockwise.reshape(sections, members, group_width, members, group_width)  37.3 us
    unnamed x11, waiting for transfers between devices  36.8 us
    unnamed x273, local copies, waits for them, and re-layouts  24.9 us
    ppermute x4, starting transfers between devices, extended_2(): lax.ppermute(tail, axis, [(i, (i + 1) % count) for i in range(ends)])  20.9 us
    dot_general x36, matrix products, grouped_taps(): jnp.einsum(pattern, window, kernel[tap_index], preferred_element_type=jnp...  18.3 us
  transfers between devices with their start and end apart: 15, of which 3 were waited for; matrix products, arithmetic and copies ran while one was open for 42% of the time, Pallas kernels for 0%

commit v1 on v0

--- a/solution.py
+++ b/solution.py
@@ -5,6 +5,23 @@
 from jax.sharding import PartitionSpec as P
 
 GW = 16
+
+
+def tell_the_cells(target, named_axis):
+    q_n = jax.lax.axis_size(named_axis)
+    items = []
+    for t in range(q_n):
+        items.append((t, (t + 1) % q_n))
+    kept_rows = []
+    for t in range(q_n):
+        kept_rows.append((t, (t - 1) % q_n))
+    row_out, v1 = ([target], [target])
+    for _ in range(q_n // 2):
+        row_out.append(jax.lax.ppermute(row_out[-1], named_axis, items))
+    for _ in range((q_n - 1) // 2):
+        v1.append(jax.lax.ppermute(v1[-1], named_axis, kept_rows))
+    x_next = jnp.concatenate([*row_out[::-1], *v1[1:]], axis=0)
+    return jnp.roll(x_next, (jax.lax.axis_index(named_axis) - q_n // 2) * target.shape[0], axis=0)
 
 
 def extended_2(cells, sides, width):
@@ -68,7 +85,7 @@
         full_in, full_group, full_out = (
             lax.all_gather(weight_in[block_index], "shard", axis=0, tiled=True),
             lax.all_gather(weight_group[block_index], "shard", axis=0, tiled=True),
-            lax.all_gather(weight_out[block_index], "shard", axis=0, tiled=True),
+            tell_the_cells(weight_out[block_index], "shard"),
         )
         hidden_width = full_in.shape[1]
         kernel = block_kernel(full_group, hidden_width, group_width)

time: 482 us -> 490 us (1.017)
  starting transfers between devices: 32.2 us -> 38.2 us
    ppermute x0 -> x6, starting transfers between devices: none -> 5.59 us  [the longest x2 3.83 us: tell_the_cells(): v1.append(jax.lax.ppermute(v1[-1], named_axis, kept_rows))]
    unnamed x273 -> x271, local copies, waits for them, and re-layouts: 24.9 us -> 24.9 us
  transfers between devices with their start and end apart: 15 -> 21, of which waited for: 3 -> 4; matrix products, arithmetic and copies ran while one was open for 42% -> 53% of each run, Pallas kernels for 0% -> 0%
where the time goes in v1:
time: 490 us; the launch traced here: 482 us
  local copies, waits for them, and re-layouts  206 us (42%)
  waiting for transfers between devices  78.5 us (16%)
  blocking collectives  54 us (11%)
  matrix products  51 us (10%)
  starting transfers between devices  38.2 us (8%)
  other arithmetic  36.9 us (8%)
  between operations  16.6 us (3%)
    reshape x52, local copies, waits for them, and re-layouts, grouped_taps(): window = window.reshape(-1, kernel.shape[1], kernel.shape[2])  60.8 us
    squeeze x18, local copies, waits for them, and re-layouts, grouped_taps(): kernel[tap_index]  41.2 us
    psum x1, waiting for transfers between devices, body(): lax.psum(jnp.stack([entry[0] for entry in shares]).astype(jnp.bfloat16),...  40.3 us
    reshape x18, local copies, waits for them, and re-layouts, body(): blockwise.reshape(sections, members, group_width, members, group_width)  37.3 us
    unnamed x11, waiting for transfers between devices  36.8 us
    unnamed x271, local copies, waits for them, and re-layouts  24.9 us
    ppermute x4, starting transfers between devices, extended_2(): lax.ppermute(tail, axis, [(i, (i + 1) % count) for i in range(ends)])  21.4 us
    dot_general x36, matrix products, grouped_taps(): jnp.einsum(pattern, window, kernel[tap_index], preferred_element_type=jnp...  18.3 us
  transfers between devices with their start and end apart: 21, of which 4 were waited for; matrix products, arithmetic and copies ran while one was open for 53% of the time, Pallas kernels for 0%

profile of v1, /device:TPU:0, one launch (start us, length us, event | category | flops | bytes accessed | tf_op | source)
XLA Modules:
  0.0 481.8 jit_solution(7589545823959790783)
XLA Ops:
  13.7 7.6 %all-gather.1 = bf16[1,512,512]{2,1,0:T(8,128)(2,1)S(1)} all-gather(bf16[1,128,512]{2,1,0:T(8,128)(2,1)S(1)} %get-tuple-element.165), channel_id=3, replica_groups=mesh['groups'=2,'rows'=4,'shard'=4] {'shard'}, dimensions={1}, use_global_device_ids=true | all-gather | bytes 655360 | tf_op jit(solution)/shard_map/all_gather | solution.py:86
  22.1 2.1 multiply_convert_fusion.5
  26.2 5.2 %collective-permute-start = (bf16[1,1,128,512]{3,2,1,0:T(8,128)(2,1)}, bf16[1,1,128,512]{3,2,1,0:T(8,128)(2,1)}, u32[]{:S(2)}, u32[]{:S(2)}) collective-permute-start(bf16[1,1,128,512]{3,2,1,0:T(8,128)(2,1)} %get-tuple-element.163), channel_id=1, source_target_pairs={{0,4},{4,8},{8,12},{1,5},{5,9},{9,13},{2,6},{6,10},{10,14},{3,7},{... | collective-permute-start | bytes 393224 | tf_op jit(solution)/shard_map/ppermute | solution.py:35
  32.5 6.2 %all-gather = bf16[1,144,512]{2,0,1:T(2,128)(2,1)S(1)} all-gather(bf16[1,36,512]{2,0,1:T(2,128)(2,1)S(1)} %get-tuple-element.167), channel_id=2, replica_groups=mesh['groups'=2,'rows'=4,'shard'=4] {'shard'}, dimensions={1}, use_global_device_ids=true | all-gather | bytes 184320 | tf_op jit(solution)/shard_map/all_gather | solution.py:87
  41.9 6.0 %all-gather.2 = bf16[1,144,512]{2,0,1:T(2,128)(2,1)S(1)} all-gather(bf16[1,36,512]{2,0,1:T(2,128)(2,1)S(1)} %get-tuple-element.168), channel_id=4, replica_groups=mesh['groups'=2,'rows'=4,'shard'=4] {'shard'}, dimensions={1}, use_global_device_ids=true | all-gather | bytes 184320 | tf_op jit(solution)/shard_map/all_gather | solution.py:87
  51.1 9.5 %all-gather.3 = bf16[1,512,512]{2,1,0:T(8,128)(2,1)} all-gather(bf16[1,128,512]{2,1,0:T(8,128)(2,1)} %get-tuple-element.166), channel_id=5, replica_groups=mesh['groups'=2,'rows'=4,'shard'=4] {'shard'}, dimensions={1}, use_global_device_ids=true | all-gather | bytes 655360 | tf_op jit(solution)/shard_map/all_gather | solution.py:86
  60.6 4.3 broadcast_multiply_fusion.1
  65.0 8.6 %fusion.130 = (bf16[1,4,8,16,8,16]{3,2,5,4,1,0:T(8,128)(2,1)S(1)}, bf16[1,4,8,16,8,16]{3,2,5,4,1,0:T(8,128)(2,1)S(1)}, bf16[1,4,8,16,8,16]{3,2,5,4,1,0:T(8,128)(...) fusion(bf16[9,4,8,16,8,16]{3,2,5,4,1,0:T(8,128)(2,1)} %get-tupl, ...), kind=kLoop, calls=%fused_computation.301 | loop fusion | bytes 4718592 | tf_op jit(solution)/shard_map/slice | solution.py:71
  73.5 2.0 squeeze.97
  75.6 2.6 squeeze.99
  78.2 2.6 squeeze.100
  80.8 2.6 squeeze.101
  83.4 2.6 squeeze.102
  86.0 2.6 squeeze.103
  88.6 2.6 squeeze.104
  91.2 2.6 squeeze.105
  93.8 2.6 squeeze.106
  96.4 8.3 %all-gather.4 = bf16[1,512,512]{2,1,0:T(8,128)(2,1)} all-gather(bf16[1,128,512]{2,1,0:T(8,128)(2,1)} %get-tuple-element.147), channel_id=6, replica_groups=mesh['groups'=2,'rows'=4,'shard'=4] {'shard'}, dimensions={1}, use_global_device_ids=true | all-gather | bytes 655360 | tf_op jit(solution)/shard_map/all_gather | solution.py:120
  142.7 2.0 copy.447
  146.2 2.2 convolution_add_fusion.35
  151.6 5.2 %collective-permute-start.5 = (bf16[1,1,128,512]{3,2,1,0:T(8,128)(2,1)}, bf16[1,1,128,512]{3,2,1,0:T(8,128)(2,1)}, u32[]{:S(2)}, u32[]{:S(2)}) collective-permute-start(bf16[1,1,128,512]{3,2,1,0:T(8,128)(2,1)} %get-tuple-element.159), channel_id=1, source_target_pairs={{0,4},{4,8},{8,12},{1,5},{5,9},{9,13},{2,6},{6,10},{10,14},{3,7},{... | collective-permute-start | bytes 393224 | tf_op jit(solution)/shard_map/ppermute | solution.py:35
  156.8 6.9 %all-gather.5 = bf16[1,512,512]{2,1,0:T(8,128)(2,1)} all-gather(bf16[1,128,512]{2,1,0:T(8,128)(2,1)S(1)} %copy-done.93), channel_id=7, replica_groups=mesh['groups'=2,'rows'=4,'shard'=4] {'shard'}, dimensions={1}, use_global_device_ids=true | all-gather | bytes 655360 | tf_op jit(solution)/shard_map/all_gather | solution.py:120
  163.7 2.6 squeeze.109
  166.3 2.6 squeeze.111
  168.9 2.6 squeeze.112
  171.5 2.6 squeeze.113
  174.1 2.6 squeeze.114
  176.7 2.6 squeeze.115
  192.3 3.5 convert_multiply_fusion
  208.9 2.0 reshape.658
  216.8 2.0 reshape.662
  230.3 5.4 %collective-permute-start.10 = (bf16[1,1,128,512]{3,2,1,0:T(8,128)(2,1)}, bf16[1,1,128,512]{3,2,1,0:T(8,128)(2,1)}, u32[]{:S(2)}, u32[]{:S(2)}) collective-permute-start(bf16[1,1,128,512]{3,2,1,0:T(8,128)(2,1)} %copy.459), channel_id=1, source_target_pairs={{0,4},{4,8},{8,12},{1,5},{5,9},{9,13},{2,6},{6,10},{10,14},{3,7},{... | collective-permute-start | bytes 393224 | tf_op jit(solution)/shard_map/ppermute | solution.py:35
  244.7 2.0 reshape.696
  248.6 2.0 reshape.698
  268.6 2.3 pad_slice_fusion
  281.1 2.0 reshape.674
  302.1 5.6 %collective-permute-start.12 = (bf16[1,1,128,512]{3,2,1,0:T(8,128)(2,1)}, bf16[1,1,128,512]{3,2,1,0:T(8,128)(2,1)}, u32[]{:S(2)}, u32[]{:S(2)}) collective-permute-start(bf16[1,1,128,512]{3,2,1,0:T(8,128)(2,1)} %copy.463), channel_id=1, source_target_pairs={{0,4},{4,8},{8,12},{1,5},{5,9},{9,13},{2,6},{6,10},{10,14},{3,7},{... | collective-permute-start | bytes 393224 | tf_op jit(solution)/shard_map/ppermute | solution.py:35
  309.6 2.9 reshape.683
  314.4 2.9 reshape.685
  319.3 3.0 reshape.687
  324.2 2.8 reshape.689
  328.9 15.7 %multiply_reduce_fusion.9 = (bf16[4,16,8,16]{3,2,1,0:T(8,128)(2,1)}, bf16[4,16,8,16]{3,2,1,0:T(8,128)(2,1)}, bf16[4,16,8,16]{3,2,1,0:T(8,128)(2,1)S(1)}, bf16[4,...) fusion(f32[4,8,16,8,16]{4,3,2,1,0:T(8,128)} %reshape.690, ...), kind=kLoop, calls=%fused_computation.29 | loop fusion | flops 2211840 | bytes 5013760 | tf_op jit(solution)/shard_map/reduce_sum | solution.py:148
  351.9 2.3 convolution_convert_fusion.2
  369.1 9.5 %fusion.129 = (bf16[40,512]{1,0:T(8,128)(2,1)S(1)}, bf16[40,512]{1,0:T(8,128)(2,1)S(1)}) fusion(bf16[144,512]{1,0:T(8,128)(2,1)S(1)} %bitcast.536, bf16[144,512]{1,0:T(8,128)(2,1)} %bitcast.44), kind=kCustom, calls=%all-reduce-scatter.2 | all-reduce-scatter fusion | flops 163841 | bytes 377344
  380.1 4.3 collective-permute-start.14
  388.8 13.7 %reduce-scatter.21.cloned.1.call-done = bf16[128,512]{1,0:T(8,128)(2,1)} async-done(((bf16[512,512]{1,0:T(8,128)(2,1)}), bf16[128,512]{1,0:T(8,128)(2,1)}) %reduce-scatter.21.cloned.1.call-update) | async-done | bytes 131088
  404.2 23.0 %reduce-scatter.17.cloned.1.call-done = bf16[128,512]{1,0:T(8,128)(2,1)} async-done(((bf16[512,512]{1,0:T(8,128)(2,1)}), bf16[128,512]{1,0:T(8,128)(2,1)}) %reduce-scatter.17.cloned.1.call-update) | async-done | bytes 131088
  430.1 40.3 %all-reduce.12.cloned.1.call-done = (bf16[2,128,512]{1,2,0:T(8,128)(2,1)}, bf16[2,36,512]{2,1,0:T(8,128)(2,1)}, bf16[2,128,512]{1,2,0:T(8,128)(2,1)}) async-done(((bf16[2,128,512]{1,2,0:T(8,128)(2,1)}, bf16[2,36,512]{2,1,0:T(8,128)(2,1)}, bf16[2,128,512]{1,2,0:T(8,128)(2,1)}), (bf16[2,128,512]{1,2,0:T(8,128)(2,1)}, bf16[2,36,512]{2,1,0:T(8,128)(2,1)}, ...) | async-done | bytes 598032 | tf_op jit(solution)/shard_map/psum | solution.py:185
  (520 shorter events, 205.4 us)
Async XLA Ops:
  7.2 379.5 %reduce-scatter.23.cloned.1.call-start = ((), (), s32[]{:S(2)}) async-start(), calls=%async_computation.7 | async-start | bytes 655360
  9.0 173.1 %collective-permute-start.7 = (bf16[128,512]{1,0:T(8,128)(2,1)}, bf16[128,512]{1,0:T(8,128)(2,1)}, u32[]{:S(2)}, u32[]{:S(2)}) collective-permute-start(bf16[128,512]{1,0:T(8,128)(2,1)} %get-tuple-element.146), channel_id=1, source_target_pairs={{0,1},{1,2},{2,3},{3,0},{4,5},{5,6},{6,7},{7,4},{8,9},{9,10},{10,1... | collective-permute-start | bytes 393224 | tf_op jit(solution)/shard_map/ppermute | solution.py:20
  9.4 182.8 %collective-permute-start.9 = (bf16[128,512]{1,0:T(8,128)(2,1)}, bf16[128,512]{1,0:T(8,128)(2,1)}, u32[]{:S(2)}, u32[]{:S(2)}) collective-permute-start(bf16[128,512]{1,0:T(8,128)(2,1)} %get-tuple-element.146), channel_id=1, source_target_pairs={{0,3},{1,0},{2,1},{3,2},{4,7},{5,4},{6,5},{7,6},{8,11},{9,8},{10,9... | collective-permute-start | bytes 393224 | tf_op jit(solution)/shard_map/ppermute | solution.py:22
  11.4 130.1 %collective-permute-start.2 = (bf16[128,512]{1,0:T(8,128)(2,1)}, bf16[128,512]{1,0:T(8,128)(2,1)}, u32[]{:S(2)}, u32[]{:S(2)}) collective-permute-start(bf16[128,512]{1,0:T(8,128)(2,1)} %get-tuple-element.145), channel_id=1, source_target_pairs={{0,1},{1,2},{2,3},{3,0},{4,5},{5,6},{6,7},{7,4},{8,9},{9,10},{10,1... | collective-permute-start | bytes 393224 | tf_op jit(solution)/shard_map/ppermute | solution.py:20
  22.1 10.3 %copy-start.104 = (bf16[2,36,512]{2,0,1:T(2,128)(2,1)S(1)}, bf16[2,36,512]{2,0,1:T(2,128)(2,1)}, u32[]{:S(2)}) copy-start(bf16[2,36,512]{2,0,1:T(2,128)(2,1)} %param.18) | copy-start | bytes 221188
  24.1 16.3 %copy-start = (bf16[256,512]{1,0:T(8,128)(2,1)}, bf16[256,512]{1,0:T(8,128)(2,1)S(1)}, u32[]{:S(2)}) copy-start(bf16[256,512]{1,0:T(8,128)(2,1)S(1)} %get-tuple-element.171) | copy-start | bytes 786436
  24.9 79.8 %collective-permute-start.1 = (bf16[1,1,128,512]{3,2,1,0:T(8,128)(2,1)}, bf16[1,1,128,512]{3,2,1,0:T(8,128)(2,1)}, u32[]{:S(2)}, u32[]{:S(2)}) collective-permute-start(bf16[1,1,128,512]{3,2,1,0:T(8,128)(2,1)} %get-tuple-element.164), channel_id=1, source_target_pairs={{4,0},{8,4},{12,8},{5,1},{9,5},{13,9},{6,2},{10,6},{14,10},{7,3},{... | collective-permute-start | bytes 393224 | tf_op jit(solution)/shard_map/ppermute | solution.py:37
  26.2 80.5 %collective-permute-start = (bf16[1,1,128,512]{3,2,1,0:T(8,128)(2,1)}, bf16[1,1,128,512]{3,2,1,0:T(8,128)(2,1)}, u32[]{:S(2)}, u32[]{:S(2)}) collective-permute-start(bf16[1,1,128,512]{3,2,1,0:T(8,128)(2,1)} %get-tuple-element.163), channel_id=1, source_target_pairs={{0,4},{4,8},{8,12},{1,5},{5,9},{9,13},{2,6},{6,10},{10,14},{3,7},{... | collective-permute-start | bytes 393224 | tf_op jit(solution)/shard_map/ppermute | solution.py:35
  88.6 18.1 %copy-start.1 = (bf16[256,512]{1,0:T(8,128)(2,1)S(1)}, bf16[256,512]{1,0:T(8,128)(2,1)}, u32[]{:S(2)}) copy-start(bf16[256,512]{1,0:T(8,128)(2,1)} %copy-done) | copy-start | bytes 786436
  104.8 40.0 %collective-permute-start.4 = (bf16[128,512]{1,0:T(8,128)(2,1)}, bf16[128,512]{1,0:T(8,128)(2,1)}, u32[]{:S(2)}, u32[]{:S(2)}) collective-permute-start(bf16[128,512]{1,0:T(8,128)(2,1)} %get-tuple-element.145), channel_id=1, source_target_pairs={{0,3},{1,0},{2,1},{3,2},{4,7},{5,4},{6,5},{7,6},{8,11},{9,8},{10,9... | collective-permute-start | bytes 393224 | tf_op jit(solution)/shard_map/ppermute | solution.py:22
  114.3 7.1 %copy-start.80 = (bf16[1,2,128,512]{3,2,1,0:T(8,128)(2,1)S(1)}, bf16[1,2,128,512]{3,2,1,0:T(8,128)(2,1)}, u32[]{:S(2)}) copy-start(bf16[1,2,128,512]{3,2,1,0:T(8,128)(2,1)} %get-tuple-element.130) | copy-start | bytes 786436
  124.0 14.2 %copy-start.2 = (bf16[256,4,128]{0,2,1:T(8,128)(2,1)S(1)}, bf16[256,4,128]{0,2,1:T(8,128)(2,1)}, u32[]{:S(2)}) copy-start(bf16[256,4,128]{0,2,1:T(8,128)(2,1)} %copy.370) | copy-start | bytes 786436
  141.5 4.7 collective-permute-start.3
  148.4 8.4 %copy-start.93 = (bf16[1,128,512]{2,1,0:T(8,128)(2,1)S(1)}, bf16[1,128,512]{2,1,0:T(8,128)(2,1)}, u32[]{:S(2)}) copy-start(bf16[1,128,512]{2,1,0:T(8,128)(2,1)} %get-tuple-element.144) | copy-start | bytes 393220
  150.3 32.5 %collective-permute-start.6 = (bf16[1,1,128,512]{3,2,1,0:T(8,128)(2,1)}, bf16[1,1,128,512]{3,2,1,0:T(8,128)(2,1)}, u32[]{:S(2)}, u32[]{:S(2)}) collective-permute-start(bf16[1,1,128,512]{3,2,1,0:T(8,128)(2,1)} %get-tuple-element.160), channel_id=1, source_target_pairs={{4,0},{8,4},{12,8},{5,1},{9,5},{13,9},{6,2},{10,6},{14,10},{7,3},{... | collective-permute-start | bytes 393224 | tf_op jit(solution)/shard_map/ppermute | solution.py:37
  151.6 31.2 %collective-permute-start.5 = (bf16[1,1,128,512]{3,2,1,0:T(8,128)(2,1)}, bf16[1,1,128,512]{3,2,1,0:T(8,128)(2,1)}, u32[]{:S(2)}, u32[]{:S(2)}) collective-permute-start(bf16[1,1,128,512]{3,2,1,0:T(8,128)(2,1)} %get-tuple-element.159), channel_id=1, source_target_pairs={{0,4},{4,8},{8,12},{1,5},{5,9},{9,13},{2,6},{6,10},{10,14},{3,7},{... | collective-permute-start | bytes 393224 | tf_op jit(solution)/shard_map/ppermute | solution.py:35
  181.4 9.4 %copy-start.52 = (bf16[4,128,128]{1,2,0:T(8,128)(2,1)}, bf16[4,128,128]{1,2,0:T(8,128)(2,1)S(1)}, u32[]{:S(2)}) copy-start(bf16[4,128,128]{1,2,0:T(8,128)(2,1)S(1)} %squeeze.117) | copy-start | bytes 393220
  182.1 8.9 %copy-start.50 = (bf16[4,128,128]{1,2,0:T(8,128)(2,1)}, bf16[4,128,128]{1,2,0:T(8,128)(2,1)S(1)}, u32[]{:S(2)}) copy-start(bf16[4,128,128]{1,2,0:T(8,128)(2,1)S(1)} %squeeze.118) | copy-start | bytes 393220
  182.1 10.2 %collective-permute-start.8 = (bf16[128,512]{1,0:T(8,128)(2,1)}, bf16[128,512]{1,0:T(8,128)(2,1)}, u32[]{:S(2)}, u32[]{:S(2)}) collective-permute-start(bf16[128,512]{1,0:T(8,128)(2,1)} %collective-permute-done.7), channel_id=1, source_target_pairs={{0,1},{1,2},{2,3},{3,0},{4,5},{5,6},{6,7},{7,4},{8,9},{9,10},{10,1... | collective-permute-start | bytes 393224 | tf_op jit(solution)/shard_map/ppermute | solution.py:20
  195.7 7.9 %copy-start.113 = (f32[256,512]{1,0:T(8,128)}, f32[256,512]{1,0:T(8,128)S(1)}, u32[]{:S(2)}) copy-start(f32[256,512]{1,0:T(8,128)S(1)} %get-tuple-element.133) | copy-start | bytes 1572868
  228.2 27.5 %collective-permute-start.11 = (bf16[1,1,128,512]{3,2,1,0:T(8,128)(2,1)}, bf16[1,1,128,512]{3,2,1,0:T(8,128)(2,1)}, u32[]{:S(2)}, u32[]{:S(2)}) collective-permute-start(bf16[1,1,128,512]{3,2,1,0:T(8,128)(2,1)} %copy.460), channel_id=1, source_target_pairs={{4,0},{8,4},{12,8},{5,1},{9,5},{13,9},{6,2},{10,6},{14,10},{7,3},{... | collective-permute-start | bytes 393224 | tf_op jit(solution)/shard_map/ppermute | solution.py:37
  229.5 8.8 %copy-start.66 = (f32[4,128,128]{2,1,0:T(8,128)S(1)}, f32[4,128,128]{2,1,0:T(8,128)}, u32[]{:S(2)}) copy-start(f32[4,128,128]{2,1,0:T(8,128)} %fusion.77) | copy-start | bytes 786436
  230.3 25.4 %collective-permute-start.10 = (bf16[1,1,128,512]{3,2,1,0:T(8,128)(2,1)}, bf16[1,1,128,512]{3,2,1,0:T(8,128)(2,1)}, u32[]{:S(2)}, u32[]{:S(2)}) collective-permute-start(bf16[1,1,128,512]{3,2,1,0:T(8,128)(2,1)} %copy.459), channel_id=1, source_target_pairs={{0,4},{4,8},{8,12},{1,5},{5,9},{9,13},{2,6},{6,10},{10,14},{3,7},{... | collective-permute-start | bytes 393224 | tf_op jit(solution)/shard_map/ppermute | solution.py:35
  254.5 133.2 %reduce-scatter.19.cloned.1.call-start = ((), (), s32[]{:S(2)}) async-start(), calls=%async_computation.5 | async-start | bytes 655360
  260.3 4.6 copy-start.12
  261.3 4.6 copy-start.14
  263.1 4.6 copy-start.3
  281.1 7.9 %copy-start.49 = (bf16[4,128,128]{1,2,0:T(8,128)(2,1)S(1)}, bf16[4,128,128]{1,2,0:T(8,128)(2,1)}, u32[]{:S(2)}) copy-start(bf16[4,128,128]{1,2,0:T(8,128)(2,1)} %squeeze.99) | copy-start | bytes 393220
  295.2 12.5 %copy-start.74 = (f32[4,128,128]{2,1,0:T(8,128)S(1)}, f32[4,128,128]{2,1,0:T(8,128)}, u32[]{:S(2)}) copy-start(f32[4,128,128]{2,1,0:T(8,128)} %fusion.79) | copy-start | bytes 786436
  299.0 64.0 %collective-permute-start.13 = (bf16[1,1,128,512]{3,2,1,0:T(8,128)(2,1)S(1)}, bf16[1,1,128,512]{3,2,1,0:T(8,128)(2,1)}, u32[]{:S(2)}, u32[]{:S(2)}) collective-permute-start(bf16[1,1,128,512]{3,2,1,0:T(8,128)(2,1)S(1)} %copy.464), channel_id=1, source_target_pairs={{4,0},{8,4},{12,8},{5,1},{9,5},{13,9},{6,2},{10,6},{14,10},{7,3},{... | collective-permute-start | bytes 393224 | tf_op jit(solution)/shard_map/ppermute | solution.py:37
  302.1 61.0 %collective-permute-start.12 = (bf16[1,1,128,512]{3,2,1,0:T(8,128)(2,1)}, bf16[1,1,128,512]{3,2,1,0:T(8,128)(2,1)}, u32[]{:S(2)}, u32[]{:S(2)}) collective-permute-start(bf16[1,1,128,512]{3,2,1,0:T(8,128)(2,1)} %copy.463), channel_id=1, source_target_pairs={{0,4},{4,8},{8,12},{1,5},{5,9},{9,13},{2,6},{6,10},{10,14},{3,7},{... | collective-permute-start | bytes 393224 | tf_op jit(solution)/shard_map/ppermute | solution.py:35
  344.6 4.9 %copy-start.103 = (bf16[4,16,8,16]{3,2,1,0:T(8,128)(2,1)S(1)}, bf16[4,16,8,16]{3,2,1,0:T(8,128)(2,1)}, u32[]{:S(2)}) copy-start(bf16[4,16,8,16]{3,2,1,0:T(8,128)(2,1)} %get-tuple-element.87) | copy-start | bytes 49156
  344.6 5.1 %copy-start.102 = (bf16[4,16,8,16]{3,2,1,0:T(8,128)(2,1)S(1)}, bf16[4,16,8,16]{3,2,1,0:T(8,128)(2,1)}, u32[]{:S(2)}) copy-start(bf16[4,16,8,16]{3,2,1,0:T(8,128)(2,1)} %get-tuple-element.88) | copy-start | bytes 49156
  344.6 5.3 %copy-start.101 = (bf16[4,16,8,16]{3,2,1,0:T(8,128)(2,1)S(1)}, bf16[4,16,8,16]{3,2,1,0:T(8,128)(2,1)}, u32[]{:S(2)}) copy-start(bf16[4,16,8,16]{3,2,1,0:T(8,128)(2,1)} %get-tuple-element.89) | copy-start | bytes 49156
  344.6 5.5 %copy-start.100 = (bf16[4,16,8,16]{3,2,1,0:T(8,128)(2,1)S(1)}, bf16[4,16,8,16]{3,2,1,0:T(8,128)(2,1)}, u32[]{:S(2)}) copy-start(bf16[4,16,8,16]{3,2,1,0:T(8,128)(2,1)} %get-tuple-element.90) | copy-start | bytes 49156
  344.6 5.8 %copy-start.99 = (bf16[4,16,8,16]{3,2,1,0:T(8,128)(2,1)S(1)}, bf16[4,16,8,16]{3,2,1,0:T(8,128)(2,1)}, u32[]{:S(2)}) copy-start(bf16[4,16,8,16]{3,2,1,0:T(8,128)(2,1)} %get-tuple-element.91) | copy-start | bytes 49156
  344.6 6.0 %copy-start.98 = (bf16[4,16,8,16]{3,2,1,0:T(8,128)(2,1)S(1)}, bf16[4,16,8,16]{3,2,1,0:T(8,128)(2,1)}, u32[]{:S(2)}) copy-start(bf16[4,16,8,16]{3,2,1,0:T(8,128)(2,1)} %get-tuple-element.75) | copy-start | bytes 49156
  346.0 5.0 %copy-start.97 = (bf16[4,16,8,16]{3,2,1,0:T(8,128)(2,1)S(1)}, bf16[4,16,8,16]{3,2,1,0:T(8,128)(2,1)}, u32[]{:S(2)}) copy-start(bf16[4,16,8,16]{3,2,1,0:T(8,128)(2,1)} %get-tuple-element.77) | copy-start | bytes 49156
  347.2 4.7 copy-start.106
  351.0 4.7 copy-start.94
  354.2 48.3 %reduce-scatter.21.cloned.1.call-start = ((), (), s32[]{:S(2)}) async-start(), calls=%async_computation.6 | async-start | bytes 655360
  359.6 5.4 %copy-start.88 = (f32[256,512]{1,0:T(8,128)S(1)}, f32[256,512]{1,0:T(8,128)}, u32[]{:S(2)}) copy-start(f32[256,512]{1,0:T(8,128)} %get-tuple-element.172) | copy-start | bytes 1572868
  362.4 64.8 %reduce-scatter.17.cloned.1.call-start = ((), (), s32[]{:S(2)}) async-start(), calls=%async_computation.4 | async-start | bytes 655360
  365.0 19.3 %copy-start.111 = (u32[32]{0:T(128)S(1)}, u32[32]{0:T(128)}, u32[]{:S(2)}) copy-start(u32[32]{0:T(128)} %constant.150) | copy-start | bytes 388
  366.6 62.5 %copy-start.20 = (bf16[1,512,512]{2,1,0:T(8,128)(2,1)S(1)}, bf16[1,512,512]{2,1,0:T(8,128)(2,1)}, u32[]{:S(2)}) copy-start(bf16[1,512,512]{2,1,0:T(8,128)(2,1)} %copy-done.19) | copy-start | bytes 1572868
  366.6 103.8 %all-reduce.12.cloned.1.call-start = ((), (), s32[]{:S(2)}) async-start(), calls=%async_computation.8 | async-start | bytes 1212416 | tf_op jit(solution)/shard_map/psum | solution.py:185
  378.6 7.0 %collective-permute-start.15 = (bf16[12,512]{1,0:T(8,128)(2,1)S(1)}, bf16[12,512]{1,0:T(8,128)(2,1)S(1)}, u32[]{:S(2)}, u32[]{:S(2)}) collective-permute-start(bf16[12,512]{1,0:T(8,128)(2,1)S(1)} %slice.537), channel_id=1, source_target_pairs={{0,1},{1,2},{2,3},{4,5},{5,6},{6,7},{8,9},{9,10},{10,11},{12,13},{... | collective-permute-start | bytes 36872
  380.1 5.7 %collective-permute-start.14 = (bf16[12,512]{1,0:T(8,128)(2,1)S(1)}, bf16[12,512]{1,0:T(8,128)(2,1)S(1)}, u32[]{:S(2)}, u32[]{:S(2)}) collective-permute-start(bf16[12,512]{1,0:T(8,128)(2,1)S(1)} %slice.536), channel_id=1, source_target_pairs={{0,1},{1,2},{2,3},{4,5},{5,6},{6,7},{8,9},{9,10},{10,11},{12,13},{... | collective-permute-start | bytes 36872
  (90 other events, 195.5 us)
Sparse Core Ops, SparseCore 0:
  254.6 21.6 reduce-scatter.22
  354.3 22.7 reduce-scatter.18
  380.2 22.1 reduce-scatter.20
  405.5 21.6 reduce-scatter.16
  430.2 40.1 all-reduce.11
